TPU v7x, 32 devices: a whole 2x2x4 slice. The times are simulated.
32 devices in a mesh: section: 4 (over z), expert: 2 (over y), mp: 4 (over x, core).
Axes of the slice: x: 2, y: 2, z: 4, core: 2. Of those that a mesh axis runs over, the one named last changes fastest.
Arguments:
- grad_in: bfloat16 [4, 256, 3072], P('section', 'expert', 'mp'), may hold values from -6 to 6
- saved_input: bfloat16 [4, 2, 256, 3072], P('section', None, 'expert', 'mp'), may hold values from -6 to 6
- routes: int32 [4, 2, 256, 2], P('section', None, 'expert'), may hold values from 0 to 3, all different within a row; in each aligned block of 128 rows (0 to 127, 128 to 255, ..., all dimensions but the last counted through in order) at most 72 rows name the same one
- route_weights: float32 [4, 2, 256, 2], P('section', None, 'expert'), may hold values from 0.2 to 1
- plan: int32 [4, 2], P('section'), may hold values from 0 to 1, each once within a row
- up_weight: bfloat16 [4, 3072, 32768], P('section', None, ('expert', 'mp')), may hold values from -0.109375 to 0.109375
- down_weight: bfloat16 [4, 32768, 3072], P('section', ('expert', 'mp')), may hold values from -0.0625 to 0.0625
Outputs:
- passed_grad: bfloat16 [4, 256, 3072], P('section', 'expert', 'mp')
Inputs may be any that keep to these rules, and one draw needn't show every extreme that they name: `routes`: the numbers of a row differ. In each aligned block of 128 rows (the rows of one index of expert within one section and microbatch) no expert is named by more than 72 rows, and some block reaches 72. `plan`: each row is a permutation of 0 to 1.
All inputs are finite; a program needn't handle non-finite values.
Results may differ from a plain program's by a relative error of at most 0.0065.
Values may be sent and summed in bfloat16 or wider, within the bound.
A program may use at most 128 MiB of HBM per device.

v0:
```python
import jax
import jax.numpy as jnp
from jax import lax
from jax.sharding import PartitionSpec as P

EXPERTS = 4
CAPACITY = 72


def from_behind(value, axis, by):
    devices = lax.axis_size(axis)
    return lax.ppermute(value, axis, [(i, (i + by) % devices) for i in range(devices)])


def targets(route_now):
    expert_ids = jnp.arange(EXPERTS, dtype=jnp.int32)
    onehot = (route_now[:, :, None] == expert_ids[None, None, :]).astype(jnp.int32)
    counts = jnp.sum(onehot, axis=1)
    before = jnp.cumsum(counts, axis=0) - counts
    slot_pos = jnp.sum(before[:, None, :] * onehot, axis=2)
    return route_now * CAPACITY + slot_pos


def per_device(grad_in, saved_input, routes, route_weights, plan, up_weight, down_weight):
    n_expert = lax.axis_size("expert")
    n_mp = lax.axis_size("mp")
    split_size = n_expert * n_mp // EXPERTS
    quarter = grad_in.shape[2]
    width = quarter * n_mp
    up_local = up_weight[0]
    down_local = down_weight[0]
    slot_ids = jnp.arange(EXPERTS * CAPACITY, dtype=jnp.int32)
    contract_last = (((1,), (1,)), ((), ()))
    current = grad_in[0]
    for step_index in range(plan.shape[1]):
        micro_index = plan[0, step_index]
        saved_now = lax.dynamic_index_in_dim(saved_input[0], micro_index, 0, keepdims=False)
        route_now = lax.dynamic_index_in_dim(routes[0], micro_index, 0, keepdims=False)
        share_now = lax.dynamic_index_in_dim(route_weights[0], micro_index, 0, keepdims=False)
        target = targets(route_now)
        hit_mask = target[None, :, :] == slot_ids[:, None, None]
        select = jnp.any(hit_mask, axis=2).astype(jnp.bfloat16)
        saved_sent = (
            jnp.dot(select, saved_now, preferred_element_type=jnp.float32)
            .astype(jnp.bfloat16)
            .reshape(EXPERTS, CAPACITY, quarter)
        )
        grad_sent = (
            jnp.dot(select, current, preferred_element_type=jnp.float32)
            .astype(jnp.bfloat16)
            .reshape(EXPERTS, CAPACITY, quarter)
        )

        def copies(array):
            return jnp.broadcast_to(
                array[:, None], (EXPERTS, split_size, CAPACITY, quarter)
            ).reshape(EXPERTS * split_size, CAPACITY, quarter)

        saved_got, grad_got = (
            lax.all_to_all(
                copies(saved_sent), ("expert", "mp"), split_axis=0, concat_axis=0, tiled=True
            ),
            lax.all_to_all(
                copies(grad_sent), ("expert", "mp"), split_axis=0, concat_axis=0, tiled=True
            ),
        )

        def assemble(array):
            return (
                array.reshape(n_expert, n_mp, CAPACITY, quarter)
                .transpose(0, 2, 1, 3)
                .reshape(n_expert * CAPACITY, width)
            )

        saved_rows = assemble(saved_got)
        grad_rows = assemble(grad_got)
        upper_pre = jnp.dot(saved_rows, up_local, preferred_element_type=jnp.float32)
        grad_act = lax.dot_general(
            grad_rows, down_local, contract_last, preferred_element_type=jnp.float32
        )
        sigma_up = jax.nn.sigmoid(upper_pre)
        grad_pre = (grad_act * sigma_up * (1.0 + upper_pre * (1.0 - sigma_up))).astype(jnp.bfloat16)
        partial_rows = lax.dot_general(
            grad_pre, up_local, contract_last, preferred_element_type=jnp.float32
        )
        outgoing = (
            partial_rows.reshape(n_expert, CAPACITY, n_mp, quarter)
            .transpose(0, 2, 1, 3)
            .reshape(n_expert * n_mp, CAPACITY, quarter)
        )
        arrived = lax.all_to_all(
            outgoing, ("expert", "mp"), split_axis=0, concat_axis=0, tiled=True
        )
        summed = jnp.sum(arrived.reshape(EXPERTS, split_size, CAPACITY, quarter), axis=1)
        mixing = jnp.sum(jnp.where(hit_mask, share_now[None, :, :], 0.0), axis=2)
        moe_term = lax.dot_general(
            mixing,
            summed.reshape(EXPERTS * CAPACITY, quarter),
            (((0,), (0,)), ((), ())),
            precision=lax.Precision.HIGHEST,
            preferred_element_type=jnp.float32,
        )
        result = (current.astype(jnp.float32) + moe_term).astype(jnp.bfloat16)
        current = from_behind(result, "section", -1)
    return current[None]


def solution(mesh):
    placed = (
        P("section", "expert", "mp"),
        P("section", None, "expert", "mp"),
        P("section", None, "expert", None),
        P("section", None, "expert", None),
        P("section", None),
        P("section", None, ("expert", "mp")),
        P("section", ("expert", "mp"), None),
    )
    return jax.shard_map(
        per_device,
        mesh=mesh,
        in_specs=placed,
        out_specs=P("section", "expert", "mp"),
        check_vma=False,
    )
```

profile of v0, /device:TPU:0, one launch (start us, length us, event | category | flops | bytes accessed | tf_op | source)
XLA Modules:
  0.0 213.0 jit_solution(8382370402191783363)
XLA Ops:
  0.0 0.0 copy-start
  0.0 1.4 fusion.40
  5.4 0.7 fusion.36
  6.1 0.1 copy.24
  6.2 0.0 copy-start.2
  6.2 0.2 reduce_window_sum.17
  6.4 0.1 copy.26
  6.5 0.1 copy.29
  6.6 0.2 reduce_window_sum.18
  6.8 0.1 copy.31
  7.0 0.0 copy-done
  7.0 0.3 convolution_convert_fusion.2
  7.3 1.0 broadcast_in_dim.71
  8.3 5.2 %all-to-all-start.1 = ((bf16[8,72,768]{2,1,0:T(8,128)(2,1)}), bf16[8,72,768]{2,1,0:T(8,128)(2,1)S(1)}, u32[]{:S(2)}, u32[]{:S(2)}) async-start(bf16[8,72,768]{2,1,0:T(8,128)(2,1)} %bitcast.11), calls=%async_computation.1 | async-start | bytes 1769472 | tf_op jit(solution)/shard_map/all_to_all | solution.py:60
  13.4 0.0 copy-done.2
  13.4 0.3 convolution_convert_fusion.3
  13.7 13.4 %all-to-all-done.1 = bf16[8,72,768]{2,1,0:T(8,128)(2,1)S(1)} async-done(((bf16[8,72,768]{2,1,0:T(8,128)(2,1)}), bf16[8,72,768]{2,1,0:T(8,128)(2,1)S(1)}, u32[]{:S(2)}, u32[]{:S(2)}) %all-to-all-start.1) | async-done | bytes 884768 | tf_op jit(solution)/shard_map/all_to_all | solution.py:60
  27.1 1.0 broadcast_in_dim.69
  28.1 3.5 %all-to-all-start = ((bf16[8,72,768]{2,1,0:T(8,128)(2,1)}), bf16[8,72,768]{2,1,0:T(8,128)(2,1)S(1)}, u32[]{:S(2)}, u32[]{:S(2)}) async-start(bf16[8,72,768]{2,1,0:T(8,128)(2,1)} %bitcast.5), calls=%async_computation | async-start | bytes 1769472 | tf_op jit(solution)/shard_map/all_to_all | solution.py:63
  31.6 0.3 copy.28
  32.0 0.1 copy.37
  32.1 13.1 %all-to-all-done = bf16[8,72,768]{2,1,0:T(8,128)(2,1)S(1)} async-done(((bf16[8,72,768]{2,1,0:T(8,128)(2,1)}), bf16[8,72,768]{2,1,0:T(8,128)(2,1)S(1)}, u32[]{:S(2)}, u32[]{:S(2)}) %all-to-all-start) | async-done | bytes 884768 | tf_op jit(solution)/shard_map/all_to_all | solution.py:63
  45.2 0.3 copy.27
  45.5 0.1 copy.36
  45.7 11.6 %fusion.2 = f32[144,4096]{1,0:T(8,128)} fusion(bf16[144,3072]{1,0:T(8,128)(2,1)S(1)} %bitcast.122, bf16[1,3072,4096]{2,1,0:T(8,128)(2,1)} %param.12), kind=kOutput, calls=%fused_computation.2 | convolution fusion | flops 3623878656 | bytes 28409856 | tf_op jit(solution)/shard_map/dot_general | solution.py:77
  57.3 13.7 %fusion.20 = bf16[144,4096]{1,0:T(8,128)(2,1)S(1)} fusion(bf16[144,3072]{1,0:T(8,128)(2,1)S(1)} %bitcast.140, bf16[1,4096,3072]{2,1,0:T(8,128)(2,1)} %param.13, f32[144,4096]{1,0:T(8,128)} %fusion.2), kind=kOutput, calls=%fused_computation.12 | convolution fusion | flops 3629187072 | bytes 29589504 | tf_op jit(solution)/shard_map/dot_general | solution.py:78
  71.0 14.5 %fusion.41 = f32[2,72,4,768]{3,1,2,0:T(8,128)} fusion(bf16[2,72,4096,1]{2,1,3,0:T(8,128)(2,1)S(1)} %bitcast.138, bf16[4,768,4096,1]{2,1,0,3:T(8,128)(2,1)} %bitcast.117), kind=kOutput, calls=%fused_computation.53 | convolution fusion | flops 3623878656 | bytes 28114944 | tf_op jit(solution)/shard_map/dot_general | solution.py:83
  85.5 3.6 %all-to-all-start.2 = ((f32[8,72,768]{2,1,0:T(8,128)}), f32[8,72,768]{2,1,0:T(8,128)S(1)}, u32[]{:S(2)}, u32[]{:S(2)}) async-start(f32[8,72,768]{2,1,0:T(8,128)} %bitcast.119), calls=%async_computation.2 | async-start | bytes 3538944 | tf_op jit(solution)/shard_map/all_to_all | solution.py:91
  89.1 0.0 copy-start.3
  89.2 0.3 convolution_convert_fusion
  89.5 22.7 %all-to-all-done.2 = f32[8,72,768]{2,1,0:T(8,128)S(1)} async-done(((f32[8,72,768]{2,1,0:T(8,128)}), f32[8,72,768]{2,1,0:T(8,128)S(1)}, u32[]{:S(2)}, u32[]{:S(2)}) %all-to-all-start.2) | async-done | bytes 1769504 | tf_op jit(solution)/shard_map/all_to_all | solution.py:91
  112.2 1.0 broadcast_in_dim.77
  113.2 3.7 %all-to-all-start.4 = ((bf16[8,72,768]{2,1,0:T(8,128)(2,1)}), bf16[8,72,768]{2,1,0:T(8,128)(2,1)S(1)}, u32[]{:S(2)}, u32[]{:S(2)}) async-start(bf16[8,72,768]{2,1,0:T(8,128)(2,1)} %bitcast.131), calls=%async_computation.4 | async-start | bytes 1769472 | tf_op jit(solution)/shard_map/all_to_all | solution.py:60
  116.9 0.0 copy-done.3
  117.0 0.1 bitcast_reduce_fusion.1
  117.1 0.8 fusion.26
  117.9 3.7 %collective-permute-start = (bf16[128,768]{1,0:T(8,128)(2,1)S(1)}, bf16[128,768]{1,0:T(8,128)(2,1)S(1)}, u32[]{:S(2)}, u32[]{:S(2)}) collective-permute-start(bf16[128,768]{1,0:T(8,128)(2,1)S(1)} %fusion.26), channel_id=1, source_target_pairs={{0,24},{8,0},{16,8},{24,16},{1,25},{9,1},{17,9},{25,17},{2,26},{10... | collective-permute-start | bytes 589832 | tf_op jit(solution)/shard_map/ppermute | solution.py:12
  121.6 8.7 %all-to-all-done.4 = bf16[8,72,768]{2,1,0:T(8,128)(2,1)S(1)} async-done(((bf16[8,72,768]{2,1,0:T(8,128)(2,1)}), bf16[8,72,768]{2,1,0:T(8,128)(2,1)S(1)}, u32[]{:S(2)}, u32[]{:S(2)}) %all-to-all-start.4) | async-done | bytes 884768 | tf_op jit(solution)/shard_map/all_to_all | solution.py:60
  130.3 0.3 copy.33
  130.7 0.1 copy.39
  130.8 0.0 collective-permute-done
  130.8 0.3 convolution_convert_fusion.1
  131.1 1.0 broadcast_in_dim.75
  132.0 3.5 %all-to-all-start.3 = ((bf16[8,72,768]{2,1,0:T(8,128)(2,1)}), bf16[8,72,768]{2,1,0:T(8,128)(2,1)S(1)}, u32[]{:S(2)}, u32[]{:S(2)}) async-start(bf16[8,72,768]{2,1,0:T(8,128)(2,1)} %bitcast.28), calls=%async_computation.3 | async-start | bytes 1769472 | tf_op jit(solution)/shard_map/all_to_all | solution.py:63
  135.6 11.6 %fusion = f32[144,4096]{1,0:T(8,128)} fusion(bf16[144,3072]{1,0:T(8,128)(2,1)S(1)} %bitcast.121, bf16[1,3072,4096]{2,1,0:T(8,128)(2,1)} %param.12), kind=kOutput, calls=%fused_computation | convolution fusion | flops 3623878656 | bytes 28409856 | tf_op jit(solution)/shard_map/dot_general | solution.py:77
  147.2 2.0 all-to-all-done.3
  149.2 0.3 copy.32
  149.5 0.1 copy.38
  149.6 13.7 %fusion.23 = bf16[144,4096]{1,0:T(8,128)(2,1)S(1)} fusion(bf16[144,3072]{1,0:T(8,128)(2,1)S(1)} %bitcast.141, bf16[1,4096,3072]{2,1,0:T(8,128)(2,1)} %param.13, f32[144,4096]{1,0:T(8,128)} %fusion), kind=kOutput, calls=%fused_computation.13 | convolution fusion | flops 3629187072 | bytes 29589504 | tf_op jit(solution)/shard_map/dot_general | solution.py:78
  163.4 14.5 %fusion.42 = f32[2,72,4,768]{3,1,2,0:T(8,128)} fusion(bf16[2,72,4096,1]{2,1,3,0:T(8,128)(2,1)S(1)} %bitcast.139, bf16[4,768,4096,1]{2,1,0,3:T(8,128)(2,1)} %bitcast.118), kind=kOutput, calls=%fused_computation.54 | convolution fusion | flops 3623878656 | bytes 28114944 | tf_op jit(solution)/shard_map/dot_general | solution.py:83
  177.9 3.6 %all-to-all-start.5 = ((f32[8,72,768]{2,1,0:T(8,128)}), f32[8,72,768]{2,1,0:T(8,128)S(1)}, u32[]{:S(2)}, u32[]{:S(2)}) async-start(f32[8,72,768]{2,1,0:T(8,128)} %bitcast.120), calls=%async_computation.5 | async-start | bytes 3538944 | tf_op jit(solution)/shard_map/all_to_all | solution.py:91
  181.5 0.0 copy-start.1
  181.5 23.0 %all-to-all-done.5 = f32[8,72,768]{2,1,0:T(8,128)S(1)} async-done(((f32[8,72,768]{2,1,0:T(8,128)}), f32[8,72,768]{2,1,0:T(8,128)S(1)}, u32[]{:S(2)}, u32[]{:S(2)}) %all-to-all-start.5) | async-done | bytes 1769504 | tf_op jit(solution)/shard_map/all_to_all | solution.py:91
  204.5 0.1 bitcast_reduce_fusion
  204.6 0.8 add_convert_fusion
  205.5 3.7 %collective-permute-start.1 = (bf16[128,768]{1,0:T(8,128)(2,1)S(1)}, bf16[128,768]{1,0:T(8,128)(2,1)S(1)}, u32[]{:S(2)}, u32[]{:S(2)}) collective-permute-start(bf16[128,768]{1,0:T(8,128)(2,1)S(1)} %add_convert_fusion), channel_id=1, source_target_pairs={{0,24},{8,0},{16,8},{24,16},{1,25},{9,1},{17,9},{25,17},{2,26},{10... | collective-permute-start | bytes 589832 | tf_op jit(solution)/shard_map/ppermute | solution.py:12
  209.1 3.2 %collective-permute-done.1 = bf16[128,768]{1,0:T(8,128)(2,1)S(1)} collective-permute-done((bf16[128,768]{1,0:T(8,128)(2,1)S(1)}, bf16[128,768]{1,0:T(8,128)(2,1)S(1)}, u32[]{:S(2)}, u32[]{:S(2)}) %collective-permute-start.1) | collective-permute-done | bytes 196640 | tf_op jit(solution)/shard_map/ppermute | solution.py:12
  212.3 0.7 copy.41
  213.0 0.0 copy-done.1
  (12 shorter events, 0.2 us)
Async XLA Ops:
  0.0 7.0 %copy-start = (bf16[1,2,128,768]{3,2,1,0:T(8,128)(2,1)S(1)}, bf16[1,2,128,768]{3,2,1,0:T(8,128)(2,1)}, u32[]{:S(2)}) copy-start(bf16[1,2,128,768]{3,2,1,0:T(8,128)(2,1)} %param.8) | copy-start | bytes 1179652
  6.2 7.2 %copy-start.2 = (bf16[1,128,768]{2,1,0:T(8,128)(2,1)S(1)}, bf16[1,128,768]{2,1,0:T(8,128)(2,1)}, u32[]{:S(2)}) copy-start(bf16[1,128,768]{2,1,0:T(8,128)(2,1)} %param.7) | copy-start | bytes 589828
  8.3 18.8 %all-to-all-start.1 = ((bf16[8,72,768]{2,1,0:T(8,128)(2,1)}), bf16[8,72,768]{2,1,0:T(8,128)(2,1)S(1)}, u32[]{:S(2)}, u32[]{:S(2)}) async-start(bf16[8,72,768]{2,1,0:T(8,128)(2,1)} %bitcast.11), calls=%async_computation.1 | async-start | bytes 1769472 | tf_op jit(solution)/shard_map/all_to_all | solution.py:60
  28.1 17.1 %all-to-all-start = ((bf16[8,72,768]{2,1,0:T(8,128)(2,1)}), bf16[8,72,768]{2,1,0:T(8,128)(2,1)S(1)}, u32[]{:S(2)}, u32[]{:S(2)}) async-start(bf16[8,72,768]{2,1,0:T(8,128)(2,1)} %bitcast.5), calls=%async_computation | async-start | bytes 1769472 | tf_op jit(solution)/shard_map/all_to_all | solution.py:63
  85.5 26.7 %all-to-all-start.2 = ((f32[8,72,768]{2,1,0:T(8,128)}), f32[8,72,768]{2,1,0:T(8,128)S(1)}, u32[]{:S(2)}, u32[]{:S(2)}) async-start(f32[8,72,768]{2,1,0:T(8,128)} %bitcast.119), calls=%async_computation.2 | async-start | bytes 3538944 | tf_op jit(solution)/shard_map/all_to_all | solution.py:91
  89.1 27.8 %copy-start.3 = (f32[1,2,128,2]{2,3,1,0:T(2,128)S(1)}, f32[1,2,128,2]{2,3,1,0:T(2,128)}, u32[]{:S(2)}) copy-start(f32[1,2,128,2]{2,3,1,0:T(2,128)} %param.10) | copy-start | bytes 6148
  113.2 17.1 %all-to-all-start.4 = ((bf16[8,72,768]{2,1,0:T(8,128)(2,1)}), bf16[8,72,768]{2,1,0:T(8,128)(2,1)S(1)}, u32[]{:S(2)}, u32[]{:S(2)}) async-start(bf16[8,72,768]{2,1,0:T(8,128)(2,1)} %bitcast.131), calls=%async_computation.4 | async-start | bytes 1769472 | tf_op jit(solution)/shard_map/all_to_all | solution.py:60
  117.9 12.9 %collective-permute-start = (bf16[128,768]{1,0:T(8,128)(2,1)S(1)}, bf16[128,768]{1,0:T(8,128)(2,1)S(1)}, u32[]{:S(2)}, u32[]{:S(2)}) collective-permute-start(bf16[128,768]{1,0:T(8,128)(2,1)S(1)} %fusion.26), channel_id=1, source_target_pairs={{0,24},{8,0},{16,8},{24,16},{1,25},{9,1},{17,9},{25,17},{2,26},{10... | collective-permute-start | bytes 589832 | tf_op jit(solution)/shard_map/ppermute | solution.py:12
  132.0 17.1 %all-to-all-start.3 = ((bf16[8,72,768]{2,1,0:T(8,128)(2,1)}), bf16[8,72,768]{2,1,0:T(8,128)(2,1)S(1)}, u32[]{:S(2)}, u32[]{:S(2)}) async-start(bf16[8,72,768]{2,1,0:T(8,128)(2,1)} %bitcast.28), calls=%async_computation.3 | async-start | bytes 1769472 | tf_op jit(solution)/shard_map/all_to_all | solution.py:63
  177.9 26.7 %all-to-all-start.5 = ((f32[8,72,768]{2,1,0:T(8,128)}), f32[8,72,768]{2,1,0:T(8,128)S(1)}, u32[]{:S(2)}, u32[]{:S(2)}) async-start(f32[8,72,768]{2,1,0:T(8,128)} %bitcast.120), calls=%async_computation.5 | async-start | bytes 3538944 | tf_op jit(solution)/shard_map/all_to_all | solution.py:91
  181.5 31.5 %copy-start.1 = (bf16[1,2,128,768]{3,2,1,0:T(8,128)(2,1)S(1)}, bf16[1,2,128,768]{3,2,1,0:T(8,128)(2,1)}, u32[]{:S(2)}) copy-start(bf16[1,2,128,768]{3,2,1,0:T(8,128)(2,1)} %param.8) | copy-start | bytes 1179652
  205.5 6.8 %collective-permute-start.1 = (bf16[128,768]{1,0:T(8,128)(2,1)S(1)}, bf16[128,768]{1,0:T(8,128)(2,1)S(1)}, u32[]{:S(2)}, u32[]{:S(2)}) collective-permute-start(bf16[128,768]{1,0:T(8,128)(2,1)S(1)} %add_convert_fusion), channel_id=1, source_target_pairs={{0,24},{8,0},{16,8},{24,16},{1,25},{9,1},{17,9},{25,17},{2,26},{10... | collective-permute-start | bytes 589832 | tf_op jit(solution)/shard_map/ppermute | solution.py:12
where the time goes:
time: 214 us; the launch traced here: 213 us
  waiting for transfers between devices  86.1 us (40%)
  matrix products  82.4 us (39%)
  starting transfers between devices  30.5 us (14%)
  local copies, waits for them, and re-layouts  8.91 us (4%)
  between operations  4.32 us (2%)
    all_to_all x2, waiting for transfers between devices, per_device(): lax.all_to_all(outgoing, ('expert', 'mp'), split_axis=0, concat_axis=0, t...  45.7 us
    dot_general x2, matrix products, per_device(): lax.dot_general(grad_pre, up_local, contract_last, preferred_element_type...  29 us
    dot_general x2, matrix products, per_device(): lax.dot_general(grad_rows, down_local, contract_last, preferred_element_t...  27.5 us
    dot_general x2, matrix products, per_device(): jnp.dot(saved_rows, up_local, preferred_element_type=jnp.float32)  23.3 us
    all_to_all x2, waiting for transfers between devices, per_device(): lax.all_to_all(copies(saved_sent), ('expert', 'mp'), split_axis=0, concat...  22.1 us
    all_to_all x2, waiting for transfers between devices, per_device(): lax.all_to_all(copies(grad_sent), ('expert', 'mp'), split_axis=0, concat_...  15.1 us
    all_to_all x2, starting transfers between devices, per_device(): lax.all_to_all(copies(saved_sent), ('expert', 'mp'), split_axis=0, concat...  8.9 us
    ppermute x2, starting transfers between devices, from_behind(): lax.ppermute(value, axis, [(i, (i + by) % devices) for i in range(devices)])  7.31 us
  transfers between devices with their start and end apart: 8, of which 7 were waited for; matrix products, arithmetic and copies ran while one was open for 7% of the time, Pallas kernels for 0%

commit v1 on v0

--- a/solution.py
+++ b/solution.py
@@ -1,10 +1,303 @@
 import jax
 import jax.numpy as jnp
 from jax import lax
+from jax.experimental import pallas as pl
+from jax.experimental.pallas import tpu as pltpu
 from jax.sharding import PartitionSpec as P
 
 EXPERTS = 4
 CAPACITY = 72
+SLOTS = 80
+HIDDEN_STEP = 512
+FEATURE_STEP = 256
+LAST_WITH_LAST = (((1,), (1,)), ((), ()))
+
+
+def fused_kernel(n_section, grad_ref, saved_ref, routes_ref, shares_ref, plan_ref, up_hbm, down_hbm, out_ref,
+                 up, down, saved_rows, grad_rows, factor, pre_grad, sent, part_out, part_in, branch_out, arrived,
+                 result, passed, weight_sem, hop_send, hop_recv, twin_send, twin_recv, part_send, part_recv,
+                 back_send, back_recv, pass_send, pass_recv):
+    section, y, mp = lax.axis_index("section"), lax.axis_index("expert"), lax.axis_index("mp")
+    x, core = mp // 2, mp % 2
+    quarter = grad_ref.shape[1]
+    hidden = up.shape[1]
+    steps = hidden // HIDDEN_STEP
+    twin = (section, y, x * 2 + 1 - core)
+    before = (lax.rem(section + n_section - 1, n_section), y, mp)
+    behind = (lax.rem(section + 1, n_section), y, mp)
+
+    def chip(k):
+        return lax.rem(y + k // 2, 2), lax.rem(x + k % 2, 2)
+
+    def peer(k):
+        py, px = chip(k)
+        return (section, py, px * 2 + core)
+
+    def place(py, px, pcore):
+        return (pl.ds(pl.multiple_of(py * SLOTS, SLOTS), SLOTS),
+                pl.ds(pl.multiple_of((px * 2 + pcore) * quarter, quarter), quarter))
+
+    def slot_rows(py, px):
+        return pl.ds(pl.multiple_of((py * 2 + px) * SLOTS, SLOTS), SLOTS)
+
+    def up_copy(i):
+        cols = pl.ds(pl.multiple_of(i * HIDDEN_STEP, HIDDEN_STEP), HIDDEN_STEP)
+        return pltpu.make_async_copy(up_hbm.at[0, :, cols], up.at[:, cols], weight_sem.at[0, i])
+
+    def down_copy(i):
+        rows = pl.ds(pl.multiple_of(i * HIDDEN_STEP, HIDDEN_STEP), HIDDEN_STEP)
+        return pltpu.make_async_copy(down_hbm.at[0, rows, :], down.at[rows, :], weight_sem.at[1, i])
+
+    def start_weights(i, carry):
+        up_copy(i).start()
+        return carry
+
+    def start_weights_down(i, carry):
+        down_copy(i).start()
+        return carry
+
+    lax.fori_loop(0, steps, start_weights, 0)
+    lax.fori_loop(0, steps, start_weights_down, 0)
+
+    barrier = pltpu.get_barrier_semaphore()
+    partners = [twin, peer(1), peer(2), peer(3), before, behind]
+    for partner in partners:
+        pl.semaphore_signal(barrier, inc=1, device_id=partner, device_id_type=pl.DeviceIdType.MESH)
+
+    tokens = routes_ref.shape[1]
+    lanes = lax.broadcasted_iota(jnp.int32, (tokens, 128), 1)
+    earlier = (lax.broadcasted_iota(jnp.int32, (tokens, tokens), 1)
+               < lax.broadcasted_iota(jnp.int32, (tokens, tokens), 0)).astype(jnp.float32).astype(jnp.bfloat16)
+    slot_ids = lax.broadcasted_iota(jnp.int32, (tokens, EXPERTS * SLOTS), 1).astype(jnp.float32)
+
+    def micro_is_second(tick):
+        return plan_ref[0:1, tick:tick + 1] == 1
+
+    def routing(tick):
+        second = jnp.broadcast_to(micro_is_second(tick), (tokens, 2))
+        route = jnp.where(second, routes_ref[1], routes_ref[0])
+        share = jnp.where(second, shares_ref[1], shares_ref[0])
+        hits = [(lanes == route[:, k:k + 1]).astype(jnp.float32) for k in range(2)]
+        counts = hits[0] + hits[1]
+        ahead = jnp.dot(earlier, counts.astype(jnp.bfloat16), preferred_element_type=jnp.float32)
+        mix = jnp.zeros((tokens, EXPERTS * SLOTS), jnp.float32)
+        select = jnp.zeros((tokens, EXPERTS * SLOTS), jnp.float32)
+        for k in range(2):
+            target = route[:, k:k + 1].astype(jnp.float32) * SLOTS + jnp.sum(ahead * hits[k], axis=1, keepdims=True)
+            here = slot_ids == target
+            mix = jnp.where(here, share[:, k:k + 1], mix)
+            select = jnp.where(here, 1.0, select)
+        high = mix.astype(jnp.bfloat16)
+        low = (mix - high.astype(jnp.float32)).astype(jnp.bfloat16)
+        return jnp.transpose(select).astype(jnp.bfloat16), high, low
+
+    def saved_of(tick):
+        second = jnp.broadcast_to(micro_is_second(tick), saved_ref.shape[1:])
+        return jnp.where(second, saved_ref[1], saved_ref[0])
+
+    def hop(number, slot, buffer, k):
+        rows, cols = place(y, x, core)
+        return pltpu.make_async_remote_copy(
+            src_ref=sent.at[slot, slot_rows(*chip(k)), :], dst_ref=buffer.at[rows, cols],
+            send_sem=hop_send.at[number, k - 1], recv_sem=hop_recv.at[number, k - 1],
+            device_id=peer(k), device_id_type=pl.DeviceIdType.MESH)
+
+    def to_twin(number, slot, buffer, k):
+        rows, cols = place(*chip(k), core)
+        source = sent.at[slot, slot_rows(y, x), :] if k == 0 else buffer.at[rows, cols]
+        return pltpu.make_async_remote_copy(
+            src_ref=source, dst_ref=buffer.at[rows, cols],
+            send_sem=twin_send.at[number, k], recv_sem=twin_recv.at[number, k],
+            device_id=twin, device_id_type=pl.DeviceIdType.MESH)
+
+    def send_rows(number, slot, buffer, select, data):
+        sent[slot] = jnp.dot(select, data, preferred_element_type=jnp.float32).astype(jnp.bfloat16)
+        for k in (3, 1, 2):
+            hop(number, slot, buffer, k).start()
+        to_twin(number, slot, buffer, 0).start()
+        rows, cols = place(y, x, core)
+        buffer[rows, cols] = sent[slot, slot_rows(y, x), :]
+
+    def relay_rows(number, slot, buffer):
+        for k in (1, 2, 3):
+            hop(number, slot, buffer, k).wait_recv()
+            to_twin(number, slot, buffer, k).start()
+
+    def finish_rows(number, slot, buffer):
+        for k in range(4):
+            to_twin(number, slot, buffer, k).wait_recv()
+        for k in range(4):
+            to_twin(number, slot, buffer, k).wait_send()
+        for k in (1, 2, 3):
+            hop(number, slot, buffer, k).wait_send()
+
+    def factor_steps(tick, first, last):
+        def body(i, carry):
+            if tick == 0:
+                up_copy(i).wait()
+            cols = pl.ds(pl.multiple_of(i * HIDDEN_STEP, HIDDEN_STEP), HIDDEN_STEP)
+            pre = jnp.dot(saved_rows[tick], up[:, cols], preferred_element_type=jnp.float32)
+            sg = 1.0 / (1.0 + jnp.exp(-pre))
+            factor[:, cols] = sg * (1.0 + pre * (1.0 - sg))
+            return carry
+        lax.fori_loop(first, last, body, 0)
+
+    def pre_grad_steps(tick):
+        def body(i, carry):
+            if tick == 0:
+                down_copy(i).wait()
+            cols = pl.ds(pl.multiple_of(i * HIDDEN_STEP, HIDDEN_STEP), HIDDEN_STEP)
+            act = lax.dot_general(grad_rows[...], down[cols, :], LAST_WITH_LAST, preferred_element_type=jnp.float32)
+            pre_grad[:, cols] = (act * factor[:, cols]).astype(jnp.bfloat16)
+            return carry
+        lax.fori_loop(0, steps, body, 0)
+
+    def branch_steps(quarter_id, store):
+        def body(i, carry):
+            start = pl.multiple_of(i * FEATURE_STEP, FEATURE_STEP)
+            rows = pl.ds(pl.multiple_of(quarter_id * quarter + start, FEATURE_STEP), FEATURE_STEP)
+            store(pl.ds(start, FEATURE_STEP),
+                  lax.dot_general(pre_grad[...], up[rows, :], LAST_WITH_LAST, preferred_element_type=jnp.float32))
+            return carry
+        lax.fori_loop(0, quarter // FEATURE_STEP, body, 0)
+
+    def part(tick, i):
+        return pltpu.make_async_remote_copy(
+            src_ref=part_out.at[i], dst_ref=part_in.at[i],
+            send_sem=part_send.at[tick, i], recv_sem=part_recv.at[tick, i],
+            device_id=twin, device_id_type=pl.DeviceIdType.MESH)
+
+    def back(tick, k):
+        py, _ = chip(k)
+        return pltpu.make_async_remote_copy(
+            src_ref=branch_out.at[k % 2, pl.ds(pl.multiple_of(py * SLOTS, SLOTS), SLOTS), :],
+            dst_ref=arrived.at[slot_rows(y, x), :],
+            send_sem=back_send.at[tick, k - 1], recv_sem=back_recv.at[tick, k - 1],
+            device_id=peer(k), device_id_type=pl.DeviceIdType.MESH)
+
+    def branches(tick):
+        for i in (1, 0):
+            px = lax.rem(x + i, 2)
+
+            def store_out(cols, value, i=i):
+                part_out[i, :, cols] = value
+
+            branch_steps(px * 2 + 1 - core, store_out)
+            part(tick, i).start()
+        for i in (1, 0):
+            px = lax.rem(x + i, 2)
+            part(tick, i).wait_recv()
+
+            def store_sum(cols, value, i=i):
+                branch_out[i, :, cols] = (value + part_in[i, :, cols]).astype(jnp.bfloat16)
+
+            branch_steps(px * 2 + core, store_sum)
+            for k in ((3, 1) if i == 1 else (2,)):
+                back(tick, k).start()
+        arrived[slot_rows(y, x), :] = branch_out[0, pl.ds(pl.multiple_of(y * SLOTS, SLOTS), SLOTS), :]
+
+    def combine(tick, current, high, low):
+        for k in (3, 1, 2):
+            back(tick, k).wait_recv()
+        rows = arrived[...]
+        moe = (jnp.dot(high, rows, preferred_element_type=jnp.float32)
+               + jnp.dot(low, rows, preferred_element_type=jnp.float32))
+        result[tick] = (current.astype(jnp.float32) + moe).astype(jnp.bfloat16)
+        pass_on(tick).start()
+
+    def finish_branches(tick):
+        for i in range(2):
+            part(tick, i).wait_send()
+        for k in (1, 2, 3):
+            back(tick, k).wait_send()
+
+    def pass_on(tick):
+        return pltpu.make_async_remote_copy(
+            src_ref=result.at[tick], dst_ref=passed.at[tick],
+            send_sem=pass_send.at[tick], recv_sem=pass_recv.at[tick],
+            device_id=before, device_id_type=pl.DeviceIdType.MESH)
+
+    select0, high0, low0 = routing(0)
+    pl.semaphore_wait(barrier, len(partners))
+    send_rows(0, 0, saved_rows.at[0], select0, saved_of(0))
+    send_rows(1, 1, grad_rows, select0, grad_ref[...])
+    relay_rows(0, 0, saved_rows.at[0])
+    select1, high1, low1 = routing(1)
+    finish_rows(0, 0, saved_rows.at[0])
+    factor_steps(0, 0, steps)
+    relay_rows(1, 1, grad_rows)
+    send_rows(2, 2, saved_rows.at[1], select1, saved_of(1))
+    finish_rows(1, 1, grad_rows)
+    pre_grad_steps(0)
+    relay_rows(2, 2, saved_rows.at[1])
+    branches(0)
+    finish_rows(2, 2, saved_rows.at[1])
+    factor_steps(1, 0, steps // 4)
+    combine(0, grad_ref[...], high0, low0)
+    finish_branches(0)
+    factor_steps(1, steps // 4, 3 * steps // 4)
+    pass_on(0).wait()
+    send_rows(3, 1, grad_rows, select1, passed[0])
+    factor_steps(1, 3 * steps // 4, steps)
+    relay_rows(3, 1, grad_rows)
+    finish_rows(3, 1, grad_rows)
+    pre_grad_steps(1)
+    branches(1)
+    combine(1, passed[0], high1, low1)
+    finish_branches(1)
+    pass_on(1).wait()
+    out_ref[...] = passed[1]
+
+
+def fused(grad_in, saved_input, routes, route_weights, plan, up_weight, down_weight):
+    n_section = lax.axis_size("section")
+    tokens, quarter = grad_in.shape[1:]
+    width, hidden = up_weight.shape[1:]
+    rows = 2 * SLOTS
+    steps = hidden // HIDDEN_STEP
+    vmem = pl.BlockSpec(memory_space=pltpu.VMEM)
+    hbm = pl.BlockSpec(memory_space=pl.ANY)
+    bf16, f32 = jnp.bfloat16, jnp.float32
+    dma = pltpu.SemaphoreType.DMA
+    flops = 2 * 2 * 3 * rows * width * hidden
+
+    def body(*refs):
+        fused_kernel(n_section, *refs)
+
+    out = pl.pallas_call(
+        body,
+        out_shape=jax.ShapeDtypeStruct((tokens, quarter), bf16),
+        in_specs=[vmem, vmem, vmem, vmem, vmem, hbm, hbm],
+        out_specs=vmem,
+        scratch_shapes=[
+            pltpu.VMEM((width, hidden), bf16),
+            pltpu.VMEM((hidden, width), bf16),
+            pltpu.VMEM((2, rows, width), bf16),
+            pltpu.VMEM((rows, width), bf16),
+            pltpu.VMEM((rows, hidden), f32),
+            pltpu.VMEM((rows, hidden), bf16),
+            pltpu.VMEM((3, EXPERTS * SLOTS, quarter), bf16),
+            pltpu.VMEM((2, rows, quarter), f32),
+            pltpu.VMEM((2, rows, quarter), f32),
+            pltpu.VMEM((2, rows, quarter), bf16),
+            pltpu.VMEM((EXPERTS * SLOTS, quarter), bf16),
+            pltpu.VMEM((2, tokens, quarter), bf16),
+            pltpu.VMEM((2, tokens, quarter), bf16),
+            dma((2, steps)),
+            dma((4, 3)), dma((4, 3)),
+            dma((4, 4)), dma((4, 4)),
+            dma((2, 2)), dma((2, 2)),
+            dma((2, 3)), dma((2, 3)),
+            dma((2,)), dma((2,)),
+        ],
+        compiler_params=pltpu.CompilerParams(
+            collective_id=0, has_side_effects=True, vmem_limit_bytes=VMEM_LIMIT),
+        cost_estimate=pl.CostEstimate(flops=flops, bytes_accessed=4 * width * hidden, transcendentals=0),
+    )(grad_in[0], saved_input[0], routes[0], route_weights[0], plan, up_weight, down_weight)
+    return out[None]
+
+
+VMEM_LIMIT = 64 * 1024 * 1024
 
 
 def from_behind(value, axis, by):
@@ -106,6 +399,7 @@
 
 
 def solution(mesh):
+    small = (mesh.shape["expert"], mesh.shape["mp"]) == (2, 4) and mesh.shape["section"] > 2
     placed = (
         P("section", "expert", "mp"),
         P("section", None, "expert", "mp"),
@@ -116,7 +410,7 @@
         P("section", ("expert", "mp"), None),
     )
     return jax.shard_map(
-        per_device,
+        fused if small else per_device,
         mesh=mesh,
         in_specs=placed,
         out_specs=P("section", "expert", "mp"),

time: 214 us -> 101 us (0.47)
  Pallas kernels: 0 us -> 96.5 us
  waiting for transfers between devices: 86.1 us -> 0 us
  matrix products: 82.4 us -> 0 us
  starting transfers between devices: 30.5 us -> 0 us
  local copies, waits for them, and re-layouts: 8.91 us -> 4.55 us
  between operations: 4.32 us -> 0.01 us
    pallas_call x0 -> x1, Pallas kernels: none -> 96.5 us  [fused(): pl.pallas_call(body, out_shape=jax.ShapeDtypeStruct((tokens, quarter), bf...]
    all_to_all x6 -> x0, waiting for transfers between devices: 82.9 us -> none  [the longest x2 45.7 us: per_device(): lax.all_to_all(outgoing, ('expert', 'mp'), split_axis=0, concat_axis=0, t...]
    dot_general x12 -> x0, matrix products: 82.4 us -> none  [the longest x2 29 us: per_device(): lax.dot_general(grad_pre, up_local, contract_last, preferred_element_type...]
    all_to_all x6 -> x0, starting transfers between devices: 23.2 us -> none  [the longest x2 8.9 us: per_device(): lax.all_to_all(copies(saved_sent), ('expert', 'mp'), split_axis=0, concat...]
    ppermute x2 -> x0, starting transfers between devices: 7.31 us -> none  [from_behind(): lax.ppermute(value, axis, [(i, (i + by) % devices) for i in range(devices)])]
    broadcast_in_dim x5 -> x0, local copies, waits for them, and re-layouts: 3.93 us -> none  [the longest x4 3.92 us: copies(): jnp.broadcast_to(array[:, None], (EXPERTS, split_size, CAPACITY, quarter))]
    unnamed x13 -> x3, local copies, waits for them, and re-layouts: 1.15 us -> 4.55 us
    ppermute x2 -> x0, waiting for transfers between devices: 3.19 us -> none  [from_behind(): lax.ppermute(value, axis, [(i, (i + by) % devices) for i in range(devices)])]
  transfers between devices with their start and end apart: 8 -> 0, of which waited for: 7 -> 0; matrix products, arithmetic and copies ran while one was open for 7% -> 0% of each run, Pallas kernels for 0% -> 0%
where the time goes in v1:
time: 101 us
  Pallas kernels  96.5 us (96%)
  local copies, waits for them, and re-layouts  4.55 us (5%)
    pallas_call x1, Pallas kernels, fused(): pl.pallas_call(body, out_shape=jax.ShapeDtypeStruct((tokens, quarter), bf...  96.5 us
    unnamed x3, local copies, waits for them, and re-layouts  4.55 us

profile of v1, /device:TPU:0, one launch (start us, length us, event | category | flops | bytes accessed | tf_op | source)
XLA Modules:
  0.0 101.0 jit_solution(18315003150745857242)
XLA Ops:
  0.0 1.5 %copy.8 = s32[1,2,128,2]{3,2,1,0:T(8,128)} copy(s32[1,2,128,2]{2,3,1,0:T(2,128)} %param.9) | data formatting | bytes 4096 | tf_op args[2]
  1.5 1.5 %copy.9 = f32[1,2,128,2]{3,2,1,0:T(8,128)} copy(f32[1,2,128,2]{2,3,1,0:T(2,128)} %param.10) | data formatting | bytes 4096 | tf_op args[3]
  2.9 96.5 %shard_map.73 = bf16[128,768]{1,0:T(8,128)(2,1)} custom-call(bf16[128,768]{1,0:T(8,128)(2,1)} %bitcast.9, bf16[2,128,768]{2,1,0:T(8,128)(2,1)} %bitcast.8, s32[2,128,2]{2,1,0:T(8,128)} %bitcast.6, f32[2,128,2]{2,1,0:T(8,128)} %bitcast.7, s32[1,2]{1,0:T(1,128)} %refs_4_.1, bf16[1,3072,4096]{2,1,0:T(8,128)(2,1)} %refs_5_.1, bf16[1,4096,3072]{2,1,0:T(8,128)(2,1)} %refs_6_.1), custom_call_target="tpu_custom_call" | custom-call | flops 24159191040 | bytes 50331648 | tf_op jit(solution)/shard_map/pallas_call | solution.py:267
  99.4 1.6 %copy.11 = bf16[1,128,768]{2,1,0:T(8,128)(2,1)} copy(bf16[1,128,768]{2,1,0:T(8,128)(2,1)} %bitcast.5) | data formatting | bytes 393216

commit v2 on v1

--- a/solution.py
+++ b/solution.py
@@ -9,6 +9,7 @@
 CAPACITY = 72
 SLOTS = 80
 HIDDEN_STEP = 512
+FIRST_PIECE = 512
 FEATURE_STEP = 256
 LAST_WITH_LAST = (((1,), (1,)), ((), ()))
 
@@ -22,6 +23,7 @@
     quarter = grad_ref.shape[1]
     hidden = up.shape[1]
     steps = hidden // HIDDEN_STEP
+    pieces = ((0, FIRST_PIECE), (FIRST_PIECE, quarter - FIRST_PIECE))
     twin = (section, y, x * 2 + 1 - core)
     before = (lax.rem(section + n_section - 1, n_section), y, mp)
     behind = (lax.rem(section + 1, n_section), y, mp)
@@ -33,9 +35,13 @@
         py, px = chip(k)
         return (section, py, px * 2 + core)
 
-    def place(py, px, pcore):
+    def place(py, px, pcore, p):
+        first, size = pieces[p]
         return (pl.ds(pl.multiple_of(py * SLOTS, SLOTS), SLOTS),
-                pl.ds(pl.multiple_of((px * 2 + pcore) * quarter, quarter), quarter))
+                pl.ds(pl.multiple_of((px * 2 + pcore) * quarter + first, 256), size))
+
+    def piece(p):
+        return pl.ds(*pieces[p])
 
     def slot_rows(py, px):
         return pl.ds(pl.multiple_of((py * 2 + px) * SLOTS, SLOTS), SLOTS)
@@ -57,79 +63,83 @@
         return carry
 
     lax.fori_loop(0, steps, start_weights, 0)
-    lax.fori_loop(0, steps, start_weights_down, 0)
 
     barrier = pltpu.get_barrier_semaphore()
     partners = [twin, peer(1), peer(2), peer(3), before, behind]
     for partner in partners:
         pl.semaphore_signal(barrier, inc=1, device_id=partner, device_id_type=pl.DeviceIdType.MESH)
 
-    tokens = routes_ref.shape[1]
-    lanes = lax.broadcasted_iota(jnp.int32, (tokens, 128), 1)
-    earlier = (lax.broadcasted_iota(jnp.int32, (tokens, tokens), 1)
-               < lax.broadcasted_iota(jnp.int32, (tokens, tokens), 0)).astype(jnp.float32).astype(jnp.bfloat16)
-    slot_ids = lax.broadcasted_iota(jnp.int32, (tokens, EXPERTS * SLOTS), 1).astype(jnp.float32)
+    tokens = routes_ref.shape[2]
+    expert_ids = lax.broadcasted_iota(jnp.int32, (8, tokens), 0)
+    earlier = (lax.broadcasted_iota(jnp.int32, (tokens, tokens), 0)
+               < lax.broadcasted_iota(jnp.int32, (tokens, tokens), 1)).astype(jnp.float32).astype(jnp.bfloat16)
+    slot_ids = lax.broadcasted_iota(jnp.int32, (EXPERTS * SLOTS, tokens), 0).astype(jnp.float32)
 
     def micro_is_second(tick):
         return plan_ref[0:1, tick:tick + 1] == 1
 
     def routing(tick):
-        second = jnp.broadcast_to(micro_is_second(tick), (tokens, 2))
+        second = jnp.broadcast_to(micro_is_second(tick), (2, tokens))
         route = jnp.where(second, routes_ref[1], routes_ref[0])
         share = jnp.where(second, shares_ref[1], shares_ref[0])
-        hits = [(lanes == route[:, k:k + 1]).astype(jnp.float32) for k in range(2)]
+        hits = [(expert_ids == route[k:k + 1, :]).astype(jnp.float32) for k in range(2)]
         counts = hits[0] + hits[1]
-        ahead = jnp.dot(earlier, counts.astype(jnp.bfloat16), preferred_element_type=jnp.float32)
-        mix = jnp.zeros((tokens, EXPERTS * SLOTS), jnp.float32)
-        select = jnp.zeros((tokens, EXPERTS * SLOTS), jnp.float32)
+        ahead = jnp.dot(counts.astype(jnp.bfloat16), earlier, preferred_element_type=jnp.float32)
+        mix = jnp.zeros((EXPERTS * SLOTS, tokens), jnp.float32)
+        select = jnp.zeros((EXPERTS * SLOTS, tokens), jnp.float32)
         for k in range(2):
-            target = route[:, k:k + 1].astype(jnp.float32) * SLOTS + jnp.sum(ahead * hits[k], axis=1, keepdims=True)
+            target = route[k:k + 1, :].astype(jnp.float32) * SLOTS + jnp.sum(ahead * hits[k], axis=0, keepdims=True)
             here = slot_ids == target
-            mix = jnp.where(here, share[:, k:k + 1], mix)
+            mix = jnp.where(here, share[k:k + 1, :], mix)
             select = jnp.where(here, 1.0, select)
+        mix = jnp.transpose(mix)
         high = mix.astype(jnp.bfloat16)
         low = (mix - high.astype(jnp.float32)).astype(jnp.bfloat16)
-        return jnp.transpose(select).astype(jnp.bfloat16), high, low
+        return select.astype(jnp.bfloat16), high, low
 
     def saved_of(tick):
         second = jnp.broadcast_to(micro_is_second(tick), saved_ref.shape[1:])
         return jnp.where(second, saved_ref[1], saved_ref[0])
 
-    def hop(number, slot, buffer, k):
-        rows, cols = place(y, x, core)
+    def hop(number, slot, buffer, p, k):
+        rows, cols = place(y, x, core, p)
         return pltpu.make_async_remote_copy(
-            src_ref=sent.at[slot, slot_rows(*chip(k)), :], dst_ref=buffer.at[rows, cols],
-            send_sem=hop_send.at[number, k - 1], recv_sem=hop_recv.at[number, k - 1],
+            src_ref=sent.at[slot, slot_rows(*chip(k)), piece(p)], dst_ref=buffer.at[rows, cols],
+            send_sem=hop_send.at[number, p, k - 1], recv_sem=hop_recv.at[number, p, k - 1],
             device_id=peer(k), device_id_type=pl.DeviceIdType.MESH)
 
-    def to_twin(number, slot, buffer, k):
-        rows, cols = place(*chip(k), core)
-        source = sent.at[slot, slot_rows(y, x), :] if k == 0 else buffer.at[rows, cols]
+    def to_twin(number, slot, buffer, p, k):
+        rows, cols = place(*chip(k), core, p)
+        source = sent.at[slot, slot_rows(y, x), piece(p)] if k == 0 else buffer.at[rows, cols]
         return pltpu.make_async_remote_copy(
             src_ref=source, dst_ref=buffer.at[rows, cols],
-            send_sem=twin_send.at[number, k], recv_sem=twin_recv.at[number, k],
+            send_sem=twin_send.at[number, p, k], recv_sem=twin_recv.at[number, p, k],
             device_id=twin, device_id_type=pl.DeviceIdType.MESH)
 
-    def send_rows(number, slot, buffer, select, data):
-        sent[slot] = jnp.dot(select, data, preferred_element_type=jnp.float32).astype(jnp.bfloat16)
+    def send_rows(number, slot, buffer, p, select, data):
+        sent[slot, :, piece(p)] = jnp.dot(select, data, preferred_element_type=jnp.float32).astype(jnp.bfloat16)
         for k in (3, 1, 2):
-            hop(number, slot, buffer, k).start()
-        to_twin(number, slot, buffer, 0).start()
-        rows, cols = place(y, x, core)
-        buffer[rows, cols] = sent[slot, slot_rows(y, x), :]
-
-    def relay_rows(number, slot, buffer):
-        for k in (1, 2, 3):
-            hop(number, slot, buffer, k).wait_recv()
-            to_twin(number, slot, buffer, k).start()
-
-    def finish_rows(number, slot, buffer):
-        for k in range(4):
-            to_twin(number, slot, buffer, k).wait_recv()
-        for k in range(4):
-            to_twin(number, slot, buffer, k).wait_send()
-        for k in (1, 2, 3):
-            hop(number, slot, buffer, k).wait_send()
+            hop(number, slot, buffer, p, k).start()
+        to_twin(number, slot, buffer, p, 0).start()
+        rows, cols = place(y, x, core, p)
+        buffer[rows, cols] = sent[slot, slot_rows(y, x), piece(p)]
+
+    def relay_rows(number, slot, buffer, p):
+        for k in (2, 1, 3):
+            hop(number, slot, buffer, p, k).wait_recv()
+            to_twin(number, slot, buffer, p, k).start()
+
+    def rows_there(number, slot, buffer):
+        for p in range(2):
+            for k in range(4):
+                to_twin(number, slot, buffer, p, k).wait_recv()
+
+    def rows_gone(number, slot, buffer):
+        for p in range(2):
+            for k in range(4):
+                to_twin(number, slot, buffer, p, k).wait_send()
+            for k in (1, 2, 3):
+                hop(number, slot, buffer, p, k).wait_send()
 
     def factor_steps(tick, first, last):
         def body(i, carry):
@@ -150,16 +160,16 @@
             act = lax.dot_general(grad_rows[...], down[cols, :], LAST_WITH_LAST, preferred_element_type=jnp.float32)
             pre_grad[:, cols] = (act * factor[:, cols]).astype(jnp.bfloat16)
             return carry
-        lax.fori_loop(0, steps, body, 0)
-
-    def branch_steps(quarter_id, store):
+        lax.fori_loop(0, hidden // HIDDEN_STEP, body, 0)
+
+    def branch_steps(quarter_id, first, size, store):
         def body(i, carry):
-            start = pl.multiple_of(i * FEATURE_STEP, FEATURE_STEP)
+            start = pl.multiple_of(first + i * FEATURE_STEP, FEATURE_STEP)
             rows = pl.ds(pl.multiple_of(quarter_id * quarter + start, FEATURE_STEP), FEATURE_STEP)
             store(pl.ds(start, FEATURE_STEP),
                   lax.dot_general(pre_grad[...], up[rows, :], LAST_WITH_LAST, preferred_element_type=jnp.float32))
             return carry
-        lax.fori_loop(0, quarter // FEATURE_STEP, body, 0)
+        lax.fori_loop(0, size // FEATURE_STEP, body, 0)
 
     def part(tick, i):
         return pltpu.make_async_remote_copy(
@@ -167,12 +177,12 @@
             send_sem=part_send.at[tick, i], recv_sem=part_recv.at[tick, i],
             device_id=twin, device_id_type=pl.DeviceIdType.MESH)
 
-    def back(tick, k):
+    def back(tick, p, k):
         py, _ = chip(k)
         return pltpu.make_async_remote_copy(
-            src_ref=branch_out.at[k % 2, pl.ds(pl.multiple_of(py * SLOTS, SLOTS), SLOTS), :],
-            dst_ref=arrived.at[slot_rows(y, x), :],
-            send_sem=back_send.at[tick, k - 1], recv_sem=back_recv.at[tick, k - 1],
+            src_ref=branch_out.at[k % 2, pl.ds(pl.multiple_of(py * SLOTS, SLOTS), SLOTS), piece(p)],
+            dst_ref=arrived.at[slot_rows(y, x), piece(p)],
+            send_sem=back_send.at[tick, p, k - 1], recv_sem=back_recv.at[tick, p, k - 1],
             device_id=peer(k), device_id_type=pl.DeviceIdType.MESH)
 
     def branches(tick):
@@ -182,70 +192,98 @@
             def store_out(cols, value, i=i):
                 part_out[i, :, cols] = value
 
-            branch_steps(px * 2 + 1 - core, store_out)
+            branch_steps(px * 2 + 1 - core, 0, quarter, store_out)
             part(tick, i).start()
-        for i in (1, 0):
-            px = lax.rem(x + i, 2)
-            part(tick, i).wait_recv()
-
-            def store_sum(cols, value, i=i):
-                branch_out[i, :, cols] = (value + part_in[i, :, cols]).astype(jnp.bfloat16)
-
-            branch_steps(px * 2 + core, store_sum)
-            for k in ((3, 1) if i == 1 else (2,)):
-                back(tick, k).start()
-        arrived[slot_rows(y, x), :] = branch_out[0, pl.ds(pl.multiple_of(y * SLOTS, SLOTS), SLOTS), :]
-
-    def combine(tick, current, high, low):
-        for k in (3, 1, 2):
-            back(tick, k).wait_recv()
-        rows = arrived[...]
+        for p in range(2):
+            for i in (1, 0):
+                px = lax.rem(x + i, 2)
+                if p == 0:
+                    part(tick, i).wait_recv()
+
+                def store_sum(cols, value, i=i):
+                    branch_out[i, :, cols] = (value + part_in[i, :, cols]).astype(jnp.bfloat16)
+
+                branch_steps(px * 2 + core, *pieces[p], store_sum)
+                for k in ((3, 1) if i == 1 else (2,)):
+                    back(tick, p, k).start()
+            arrived[slot_rows(y, x), piece(p)] = branch_out[0, pl.ds(pl.multiple_of(y * SLOTS, SLOTS), SLOTS), piece(p)]
+
+    def combine(tick, p, current, high, low):
+        for k in (2, 1, 3):
+            back(tick, p, k).wait_recv()
+        rows = arrived[:, piece(p)]
         moe = (jnp.dot(high, rows, preferred_element_type=jnp.float32)
                + jnp.dot(low, rows, preferred_element_type=jnp.float32))
-        result[tick] = (current.astype(jnp.float32) + moe).astype(jnp.bfloat16)
-        pass_on(tick).start()
+        result[tick, :, piece(p)] = (current.astype(jnp.float32) + moe).astype(jnp.bfloat16)
+        pass_on(tick, p).start()
 
     def finish_branches(tick):
         for i in range(2):
             part(tick, i).wait_send()
-        for k in (1, 2, 3):
-            back(tick, k).wait_send()
-
-    def pass_on(tick):
+        for p in range(2):
+            for k in (1, 2, 3):
+                back(tick, p, k).wait_send()
+
+    def pass_on(tick, p):
         return pltpu.make_async_remote_copy(
-            src_ref=result.at[tick], dst_ref=passed.at[tick],
-            send_sem=pass_send.at[tick], recv_sem=pass_recv.at[tick],
+            src_ref=result.at[tick, :, piece(p)], dst_ref=passed.at[tick, :, piece(p)],
+            send_sem=pass_send.at[tick, p], recv_sem=pass_recv.at[tick, p],
             device_id=before, device_id_type=pl.DeviceIdType.MESH)
 
     select0, high0, low0 = routing(0)
     pl.semaphore_wait(barrier, len(partners))
-    send_rows(0, 0, saved_rows.at[0], select0, saved_of(0))
-    send_rows(1, 1, grad_rows, select0, grad_ref[...])
-    relay_rows(0, 0, saved_rows.at[0])
+    saved0, saved1 = saved_rows.at[0], saved_rows.at[1]
+    rows_of = saved_of(0)
+    for p in range(2):
+        first, size = pieces[p]
+        send_rows(0, 0, saved0, p, select0, rows_of[:, first:first + size])
+    for p in range(2):
+        relay_rows(0, 0, saved0, p)
+    lax.fori_loop(0, steps, start_weights_down, 0)
+    for p in range(2):
+        send_rows(1, 1, grad_rows, p, select0, grad_ref[:, piece(p)])
+    rows_there(0, 0, saved0)
+    factor_steps(0, 0, steps)
+    for p in range(2):
+        relay_rows(1, 1, grad_rows, p)
     select1, high1, low1 = routing(1)
-    finish_rows(0, 0, saved_rows.at[0])
-    factor_steps(0, 0, steps)
-    relay_rows(1, 1, grad_rows)
-    send_rows(2, 2, saved_rows.at[1], select1, saved_of(1))
-    finish_rows(1, 1, grad_rows)
+    rows_gone(0, 0, saved0)
+    rows_of = saved_of(1)
+    for p in range(2):
+        first, size = pieces[p]
+        send_rows(2, 0, saved1, p, select1, rows_of[:, first:first + size])
+    rows_there(1, 1, grad_rows)
     pre_grad_steps(0)
-    relay_rows(2, 2, saved_rows.at[1])
+    for p in range(2):
+        relay_rows(2, 0, saved1, p)
+    rows_gone(1, 1, grad_rows)
     branches(0)
-    finish_rows(2, 2, saved_rows.at[1])
-    factor_steps(1, 0, steps // 4)
-    combine(0, grad_ref[...], high0, low0)
+    rows_there(2, 0, saved1)
+    combine(0, 0, grad_ref[:, piece(0)], high0, low0)
+    factor_steps(1, 0, 1)
+    combine(0, 1, grad_ref[:, piece(1)], high0, low0)
+    factor_steps(1, 1, 4)
+    pass_on(0, 0).wait_recv()
+    send_rows(3, 1, grad_rows, 0, select1, passed[0, :, piece(0)])
+    factor_steps(1, 4, 5)
+    pass_on(0, 1).wait_recv()
+    send_rows(3, 1, grad_rows, 1, select1, passed[0, :, piece(1)])
+    factor_steps(1, 5, 6)
+    relay_rows(3, 1, grad_rows, 0)
+    factor_steps(1, 6, steps)
+    relay_rows(3, 1, grad_rows, 1)
     finish_branches(0)
-    factor_steps(1, steps // 4, 3 * steps // 4)
-    pass_on(0).wait()
-    send_rows(3, 1, grad_rows, select1, passed[0])
-    factor_steps(1, 3 * steps // 4, steps)
-    relay_rows(3, 1, grad_rows)
-    finish_rows(3, 1, grad_rows)
+    rows_gone(2, 0, saved1)
+    rows_there(3, 1, grad_rows)
     pre_grad_steps(1)
     branches(1)
-    combine(1, passed[0], high1, low1)
+    for p in range(2):
+        combine(1, p, passed[0, :, piece(p)], high1, low1)
+    rows_gone(3, 1, grad_rows)
     finish_branches(1)
-    pass_on(1).wait()
+    for p in range(2):
+        pass_on(0, p).wait_send()
+        pass_on(1, p).wait()
     out_ref[...] = passed[1]
 
 
@@ -276,7 +314,7 @@
             pltpu.VMEM((rows, width), bf16),
             pltpu.VMEM((rows, hidden), f32),
             pltpu.VMEM((rows, hidden), bf16),
-            pltpu.VMEM((3, EXPERTS * SLOTS, quarter), bf16),
+            pltpu.VMEM((2, EXPERTS * SLOTS, quarter), bf16),
             pltpu.VMEM((2, rows, quarter), f32),
             pltpu.VMEM((2, rows, quarter), f32),
             pltpu.VMEM((2, rows, quarter), bf16),
@@ -284,16 +322,16 @@
             pltpu.VMEM((2, tokens, quarter), bf16),
             pltpu.VMEM((2, tokens, quarter), bf16),
             dma((2, steps)),
-            dma((4, 3)), dma((4, 3)),
-            dma((4, 4)), dma((4, 4)),
+            dma((4, 2, 3)), dma((4, 2, 3)),
+            dma((4, 2, 4)), dma((4, 2, 4)),
             dma((2, 2)), dma((2, 2)),
-            dma((2, 3)), dma((2, 3)),
-            dma((2,)), dma((2,)),
+            dma((2, 2, 3)), dma((2, 2, 3)),
+            dma((2, 2)), dma((2, 2)),
         ],
         compiler_params=pltpu.CompilerParams(
             collective_id=0, has_side_effects=True, vmem_limit_bytes=VMEM_LIMIT),
         cost_estimate=pl.CostEstimate(flops=flops, bytes_accessed=4 * width * hidden, transcendentals=0),
-    )(grad_in[0], saved_input[0], routes[0], route_weights[0], plan, up_weight, down_weight)
+    )(grad_in[0], saved_input[0], routes[0].transpose(0, 2, 1), route_weights[0].transpose(0, 2, 1), plan, up_weight, down_weight)
     return out[None]
 
 

time: 101 us -> 90.1 us (0.89)
  Pallas kernels: 96.5 us -> 88.3 us
  local copies, waits for them, and re-layouts: 4.55 us -> 1.62 us
    pallas_call x1, Pallas kernels: 96.5 us -> 88.3 us  [fused(): pl.pallas_call(body, out_shape=jax.ShapeDtypeStruct((tokens, quarter), bf...]
    unnamed x3 -> x1, local copies, waits for them, and re-layouts: 4.55 us -> 1.62 us
where the time goes in v2:
time: 90.1 us; the launch traced here: 89.9 us
  Pallas kernels  88.3 us (98%)
  local copies, waits for them, and re-layouts  1.62 us (2%)
    pallas_call x1, Pallas kernels, fused(): pl.pallas_call(body, out_shape=jax.ShapeDtypeStruct((tokens, quarter), bf...  88.3 us

profile of v2, /device:TPU:0, one launch (start us, length us, event | category | flops | bytes accessed | tf_op | source)
XLA Modules:
  0.0 89.9 jit_solution(10899452771441633927)
XLA Ops:
  0.0 88.3 %shard_map.73 = bf16[128,768]{1,0:T(8,128)(2,1)} custom-call(bf16[128,768]{1,0:T(8,128)(2,1)} %bitcast.11, bf16[2,128,768]{2,1,0:T(8,128)(2,1)} %bitcast.10, s32[2,2,128]{2,1,0:T(2,128)} %bitcast.12, f32[2,2,128]{2,1,0:T(2,128)} %bitcast.13, s32[1,2]{1,0:T(1,128)} %refs_4_.1, bf16[1,3072,4096]{2,1,0:T(8,128)(2,1)} %refs_5_.1, bf16[1,4096,3072]{2,1,0:T(8,128)(2,1)} %refs_6_.1), custom_call_target="tpu_custom_call" | custom-call | flops 24159191040 | bytes 50331648 | tf_op jit(solution)/shard_map/pallas_call | solution.py:305
  88.3 1.6 %copy.9 = bf16[1,128,768]{2,1,0:T(8,128)(2,1)} copy(bf16[1,128,768]{2,1,0:T(8,128)(2,1)} %bitcast.9) | data formatting | bytes 393216

commit v3 on v2

--- a/solution.py
+++ b/solution.py
@@ -10,7 +10,6 @@
 SLOTS = 80
 HIDDEN_STEP = 512
 FIRST_PIECE = 512
-FEATURE_STEP = 256
 LAST_WITH_LAST = (((1,), (1,)), ((), ()))
 
 
@@ -160,16 +159,12 @@
             act = lax.dot_general(grad_rows[...], down[cols, :], LAST_WITH_LAST, preferred_element_type=jnp.float32)
             pre_grad[:, cols] = (act * factor[:, cols]).astype(jnp.bfloat16)
             return carry
-        lax.fori_loop(0, hidden // HIDDEN_STEP, body, 0)
-
-    def branch_steps(quarter_id, first, size, store):
-        def body(i, carry):
-            start = pl.multiple_of(first + i * FEATURE_STEP, FEATURE_STEP)
-            rows = pl.ds(pl.multiple_of(quarter_id * quarter + start, FEATURE_STEP), FEATURE_STEP)
-            store(pl.ds(start, FEATURE_STEP),
-                  lax.dot_general(pre_grad[...], up[rows, :], LAST_WITH_LAST, preferred_element_type=jnp.float32))
-            return carry
-        lax.fori_loop(0, size // FEATURE_STEP, body, 0)
+        lax.fori_loop(0, hidden // HIDDEN_STEP, body, 0, unroll=1 if tick == 0 else 2)
+
+    def branch_of(quarter_id, p):
+        first, size = pieces[p]
+        rows = pl.ds(pl.multiple_of(quarter_id * quarter + first, 256), size)
+        return lax.dot_general(pre_grad[...], up[rows, :], LAST_WITH_LAST, preferred_element_type=jnp.float32)
 
     def part(tick, i):
         return pltpu.make_async_remote_copy(
@@ -188,22 +183,16 @@
     def branches(tick):
         for i in (1, 0):
             px = lax.rem(x + i, 2)
-
-            def store_out(cols, value, i=i):
-                part_out[i, :, cols] = value
-
-            branch_steps(px * 2 + 1 - core, 0, quarter, store_out)
+            for p in range(2):
+                part_out[i, :, piece(p)] = branch_of(px * 2 + 1 - core, p).astype(jnp.bfloat16)
             part(tick, i).start()
         for p in range(2):
             for i in (1, 0):
                 px = lax.rem(x + i, 2)
                 if p == 0:
                     part(tick, i).wait_recv()
-
-                def store_sum(cols, value, i=i):
-                    branch_out[i, :, cols] = (value + part_in[i, :, cols]).astype(jnp.bfloat16)
-
-                branch_steps(px * 2 + core, *pieces[p], store_sum)
+                own = branch_of(px * 2 + core, p) + part_in[i, :, piece(p)].astype(jnp.float32)
+                branch_out[i, :, piece(p)] = own.astype(jnp.bfloat16)
                 for k in ((3, 1) if i == 1 else (2,)):
                     back(tick, p, k).start()
             arrived[slot_rows(y, x), piece(p)] = branch_out[0, pl.ds(pl.multiple_of(y * SLOTS, SLOTS), SLOTS), piece(p)]
@@ -315,8 +304,8 @@
             pltpu.VMEM((rows, hidden), f32),
             pltpu.VMEM((rows, hidden), bf16),
             pltpu.VMEM((2, EXPERTS * SLOTS, quarter), bf16),
-            pltpu.VMEM((2, rows, quarter), f32),
-            pltpu.VMEM((2, rows, quarter), f32),
+            pltpu.VMEM((2, rows, quarter), bf16),
+            pltpu.VMEM((2, rows, quarter), bf16),
             pltpu.VMEM((2, rows, quarter), bf16),
             pltpu.VMEM((EXPERTS * SLOTS, quarter), bf16),
             pltpu.VMEM((2, tokens, quarter), bf16),

time: 90.1 us -> 88.8 us (0.986)
  Pallas kernels: 88.3 us -> 87.1 us
    pallas_call x1, Pallas kernels: 88.3 us -> 87.1 us  [fused(): pl.pallas_call(body, out_shape=jax.ShapeDtypeStruct((tokens, quarter), bf...]
where the time goes in v3:
time: 88.8 us; the launch traced here: 88.7 us
  Pallas kernels  87.1 us (98%)
  local copies, waits for them, and re-layouts  1.62 us (2%)
    pallas_call x1, Pallas kernels, fused(): pl.pallas_call(body, out_shape=jax.ShapeDtypeStruct((tokens, quarter), bf...  87.1 us

profile of v3, /device:TPU:0, one launch (start us, length us, event | category | flops | bytes accessed | tf_op | source)
XLA Modules:
  0.0 88.7 jit_solution(3002162231384350266)
XLA Ops:
  0.0 87.1 %shard_map.73 = bf16[128,768]{1,0:T(8,128)(2,1)} custom-call(bf16[128,768]{1,0:T(8,128)(2,1)} %bitcast.11, bf16[2,128,768]{2,1,0:T(8,128)(2,1)} %bitcast.10, s32[2,2,128]{2,1,0:T(2,128)} %bitcast.12, f32[2,2,128]{2,1,0:T(2,128)} %bitcast.13, s32[1,2]{1,0:T(1,128)} %refs_4_.1, bf16[1,3072,4096]{2,1,0:T(8,128)(2,1)} %refs_5_.1, bf16[1,4096,3072]{2,1,0:T(8,128)(2,1)} %refs_6_.1), custom_call_target="tpu_custom_call" | custom-call | flops 24159191040 | bytes 50331648 | tf_op jit(solution)/shard_map/pallas_call | solution.py:294
  87.1 1.6 %copy.9 = bf16[1,128,768]{2,1,0:T(8,128)(2,1)} copy(bf16[1,128,768]{2,1,0:T(8,128)(2,1)} %bitcast.9) | data formatting | bytes 393216
